TPU v7x, 32 devices: a whole 2x2x4 slice. The times are simulated.
32 devices in a mesh: row: 8 (over z, x), col: 4 (over y, core).
Axes of the slice: x: 2, y: 2, z: 4, core: 2. Of those that a mesh axis runs over, the one named last changes fastest.
Arguments:
- reflection: bfloat16 [2, 8, 6144, 6144], P(None, None, 'row', 'col'), may hold values from -0.0390625 to 0.0390625
- initial: bfloat16 [96, 2, 8, 6144], P('row', None, None, 'col'), may hold values from -6 to 6
- onset_down: int32 [96, 6144], P('col', 'row'), may hold values from 4 to 27
- onset_up: int32 [96, 6144], P('row', 'col'), may hold values from 4 to 27
Outputs:
- minus_field: float32 [96, 2, 8, 6144], P('col', None, None, 'row')
- plus_field: float32 [96, 2, 8, 6144], P('row', None, None, 'col')
All inputs are finite; a program needn't handle non-finite values.
Results may differ from a plain program's by a relative error of at most 0.019.
Values may be sent and summed in bfloat16 or wider, within the bound.
A program may use at most 128 MiB of HBM per device.

v0:
```python
import math

import jax
import jax.numpy as jnp
from jax import lax
from jax.sharding import PartitionSpec as P

NT = 32
ITERS = 2


def dft_tables(freq_count, time_count):
    time_index = lax.broadcasted_iota(jnp.int32, (time_count, freq_count), 0)
    orders = lax.broadcasted_iota(jnp.int32, (time_count, freq_count), 1) + 2
    phases = time_index * orders % time_count
    angles = phases.astype(jnp.float32) * (2.0 * math.pi / time_count)
    to_time = jnp.concatenate([jnp.cos(angles), -jnp.sin(angles)], axis=1)
    to_freq = to_time.T * (2.0 / time_count)
    return (to_time, to_freq)


def window(spectra, onsets):
    to_time, to_freq = dft_tables(spectra.shape[2], NT)
    flattened = spectra.reshape(spectra.shape[0], 2 * spectra.shape[2], spectra.shape[3])
    series = jnp.einsum("tq,vqs->vts", to_time, flattened, precision=lax.Precision.HIGHEST)
    moments = lax.broadcasted_iota(jnp.int32, (1, NT, 1), 1)
    keep_mask = moments < onsets[:, None, :]
    series = jnp.where(keep_mask, series, jnp.zeros_like(series))
    spectrum = jnp.einsum("qt,vts->vqs", to_freq, series, precision=lax.Precision.HIGHEST)
    return spectrum.reshape(spectra.shape)


def forward_local(reflection, focus):
    real_part = jnp.einsum(
        "nsk,vnk->vns", reflection[0], focus[:, 0], preferred_element_type=jnp.float32
    ) - jnp.einsum("nsk,vnk->vns", reflection[1], focus[:, 1], preferred_element_type=jnp.float32)
    imag_part = jnp.einsum(
        "nsk,vnk->vns", reflection[0], focus[:, 1], preferred_element_type=jnp.float32
    ) + jnp.einsum("nsk,vnk->vns", reflection[1], focus[:, 0], preferred_element_type=jnp.float32)
    return jnp.stack([real_part, imag_part], axis=1)


def adjoint_local(reflection, moving):
    real_part = jnp.einsum(
        "nsk,vns->vnk", reflection[0], moving[:, 0], preferred_element_type=jnp.float32
    ) + jnp.einsum("nsk,vns->vnk", reflection[1], moving[:, 1], preferred_element_type=jnp.float32)
    imag_part = jnp.einsum(
        "nsk,vns->vnk", reflection[0], moving[:, 1], preferred_element_type=jnp.float32
    ) - jnp.einsum("nsk,vns->vnk", reflection[1], moving[:, 0], preferred_element_type=jnp.float32)
    return jnp.stack([real_part, imag_part], axis=1)


def body(reflection, initial, onset_down, onset_up):
    initial_all = lax.all_gather(initial, "row", axis=0, tiled=True)
    focus_low = initial_all
    minus_field = None
    plus_field = None
    for iteration in range(ITERS):
        focus = focus_low
        summed = lax.psum_scatter(
            forward_local(reflection, focus).astype(jnp.bfloat16),
            "col",
            scatter_dimension=0,
            tiled=True,
        ).astype(jnp.float32)
        minus_field = window(summed, onset_down)
        moving_all = lax.all_gather(minus_field.astype(jnp.bfloat16), "col", axis=0, tiled=True)
        summed_up = lax.psum_scatter(
            adjoint_local(reflection, moving_all).astype(jnp.bfloat16),
            "row",
            scatter_dimension=0,
            tiled=True,
        ).astype(jnp.float32)
        plus_field = initial.astype(jnp.float32) + window(summed_up, onset_up)
        if iteration + 1 < ITERS:
            focus_low = lax.all_gather(plus_field.astype(jnp.bfloat16), "row", axis=0, tiled=True)
    return (minus_field, plus_field)


def solution(mesh):
    return jax.shard_map(
        body,
        mesh=mesh,
        in_specs=(
            P(None, None, "row", "col"),
            P("row", None, None, "col"),
            P("col", "row"),
            P("row", "col"),
        ),
        out_specs=(P("col", None, None, "row"), P("row", None, None, "col")),
        check_vma=False,
    )
```

profile of v0, /device:TPU:0, one launch (start us, length us, event | category | flops | bytes accessed | tf_op | source)
XLA Modules:
  0.0 677.7 jit_solution(5853695715045226913)
XLA Ops:
  7.2 0.7 all-gather.5.cloned.1.call-update
  7.9 84.8 %all-gather.5.cloned.1.call-done = bf16[96,2,8,1536]{3,2,1,0:T(8,128)(2,1)} async-done(((bf16[12,2,8,1536]{3,2,1,0:T(8,128)(2,1)}), bf16[96,2,8,1536]{3,2,1,0:T(8,128)(2,1)}) %all-gather.5.cloned.1.call-update) | async-done | bytes 4718608 | tf_op jit(solution)/shard_map/all_gather | solution.py:54
  92.8 2.7 fusion.138
  95.5 11.3 %fusion.14 = f32[8,96,768]{2,1,0:T(8,128)} fusion(bf16[2,8,768,1536]{3,2,1,0:T(8,128)(2,1)} %param.4, bf16[96,1,8,1536]{3,2,1,0:T(8,128)(2,1)S(1)} %get-tuple-element.6), kind=kOutput, calls=%fused_computation.14 | convolution fusion | flops 1811939328 | bytes 23592960 | tf_op jit(solution)/shard_map/nsk,vnk->vns/dot_general | solution.py:36
  106.7 11.3 %fusion.12 = f32[8,96,768]{2,1,0:T(8,128)} fusion(bf16[2,8,768,1536]{3,2,1,0:T(8,128)(2,1)} %param.4, bf16[96,1,8,1536]{3,2,1,0:T(8,128)(2,1)S(1)} %get-tuple-element.7), kind=kOutput, calls=%fused_computation.12 | convolution fusion | flops 1811939328 | bytes 23592960 | tf_op jit(solution)/shard_map/nsk,vnk->vns/dot_general | solution.py:39
  118.0 10.8 %fusion.78 = bf16[96,1,8,768]{3,0,2,1:T(8,128)(2,1)S(1)} fusion(f32[8,96,768]{2,1,0:T(8,128)} %fusion.14, bf16[2,8,768,1536]{3,2,1,0:T(8,128)(2,1)} %param.4, bf16[96,1,8,1536]{3,2,1,0:T(8,128)(2,1)S(1)} %get-tuple-element.7), kind=kOutput, calls=%fused_computation.84 | convolution fusion | flops 1813118976 | bytes 24772608 | tf_op jit(solution)/shard_map/nsk,vnk->vns/dot_general | solution.py:34
  128.8 10.8 %fusion.83 = bf16[96,1,8,768]{3,0,2,1:T(8,128)(2,1)S(1)} fusion(f32[8,96,768]{2,1,0:T(8,128)} %fusion.12, bf16[2,8,768,1536]{3,2,1,0:T(8,128)(2,1)} %param.4, bf16[96,1,8,1536]{3,2,1,0:T(8,128)(2,1)S(1)} %get-tuple-element.6), kind=kOutput, calls=%fused_computation.85 | convolution fusion | flops 1813118976 | bytes 24772608 | tf_op jit(solution)/shard_map/nsk,vnk->vns/dot_general | solution.py:37
  139.8 1.6 copy.33
  141.5 0.3 all-gather.7.cloned.1.call-start
  141.9 31.0 %reduce-scatter.13.cloned.1.call-done = bf16[24,12288]{1,0:T(8,128)(2,1)} async-done(((bf16[96,12288]{1,0:T(8,128)(2,1)}), bf16[24,12288]{1,0:T(8,128)(2,1)}) %reduce-scatter.13.cloned.1.call-update) | async-done | bytes 589840
  172.8 1.2 copy.34
  174.0 1.1 fusion.104
  175.2 1.6 fusion.97
  176.7 1.0 copy.15
  177.8 24.2 %all-gather.7.cloned.1.call-done = bf16[96,2,8,768]{3,0,2,1:T(8,128)(2,1)} async-done(((bf16[24,2,8,768]{3,0,2,1:T(8,128)(2,1)}), bf16[96,2,8,768]{3,0,2,1:T(8,128)(2,1)}) %all-gather.7.cloned.1.call-update) | async-done | bytes 2359312 | tf_op jit(solution)/shard_map/all_gather | solution.py:67
  202.0 8.4 %fusion.8 = f32[8,96,1536]{2,1,0:T(8,128)S(1)} fusion(bf16[2,8,768,1536]{3,2,1,0:T(8,128)(2,1)} %param.4, bf16[96,2,8,768]{3,0,2,1:T(8,128)(2,1)} %all-gather.7.cloned.1.call-done), kind=kOutput, calls=%fused_computation.8 | convolution fusion | flops 1811939328 | bytes 24772608 | tf_op jit(solution)/shard_map/nsk,vns->vnk/dot_general | solution.py:49
  210.4 8.4 %fusion.10 = f32[8,96,1536]{2,1,0:T(8,128)S(1)} fusion(bf16[2,8,768,1536]{3,2,1,0:T(8,128)(2,1)} %param.4, bf16[96,2,8,768]{3,0,2,1:T(8,128)(2,1)} %all-gather.7.cloned.1.call-done), kind=kOutput, calls=%fused_computation.10 | convolution fusion | flops 1811939328 | bytes 24772608 | tf_op jit(solution)/shard_map/nsk,vns->vnk/dot_general | solution.py:46
  218.8 8.5 %fusion.59 = bf16[96,1,8,1536]{3,0,2,1:T(8,128)(2,1)S(1)} fusion(f32[8,96,1536]{2,1,0:T(8,128)S(1)} %fusion.8, bf16[2,8,768,1536]{3,2,1,0:T(8,128)(2,1)} %param.4, bf16[96,2,8,768]{3,0,2,1:T(8,128)(2,1)} %all-gather.7.cloned.1.call-done), kind=kOutput, calls=%fused_computation.55 | convolution fusion | flops 1814298624 | bytes 27131904 | tf_op jit(solution)/shard_map/nsk,vns->vnk/dot_general | solution.py:47
  227.2 8.5 %fusion.56 = bf16[96,1,8,1536]{3,0,2,1:T(8,128)(2,1)S(1)} fusion(f32[8,96,1536]{2,1,0:T(8,128)S(1)} %fusion.10, bf16[2,8,768,1536]{3,2,1,0:T(8,128)(2,1)} %param.4, bf16[96,2,8,768]{3,0,2,1:T(8,128)(2,1)} %all-gather.7.cloned.1.call-done), kind=kOutput, calls=%fused_computation.54 | convolution fusion | flops 1814298624 | bytes 27131904 | tf_op jit(solution)/shard_map/nsk,vns->vnk/dot_general | solution.py:44
  235.7 0.4 pad_maximum_fusion
  236.1 4.7 copy.16
  240.9 0.5 all-gather.9.cloned.1.call-start
  241.4 94.9 %reduce-scatter.9.cloned.1.call-done = bf16[12,2,8,1536]{3,2,1,0:T(8,128)(2,1)} async-done(((bf16[96,2,8,1536]{3,2,1,0:T(8,128)(2,1)}), bf16[12,2,8,1536]{3,2,1,0:T(8,128)(2,1)}) %reduce-scatter.9.cloned.1.call-update) | async-done | bytes 589840 | tf_op jit(solution)/shard_map/reduce_scatter | solution.py:68
  336.3 2.4 fusion.69
  338.7 2.3 fusion.72
  341.1 79.7 %all-gather.9.cloned.1.call-done = bf16[96,2,8,1536]{3,2,1,0:T(8,128)(2,1)} async-done(((bf16[12,2,8,1536]{3,2,1,0:T(8,128)(2,1)}), bf16[96,2,8,1536]{3,2,1,0:T(8,128)(2,1)}) %all-gather.9.cloned.1.call-update) | async-done | bytes 4718608 | tf_op jit(solution)/shard_map/all_gather | solution.py:76
  420.8 2.7 fusion.137
  423.5 11.3 %fusion.6 = f32[8,96,768]{2,1,0:T(8,128)} fusion(bf16[2,8,768,1536]{3,2,1,0:T(8,128)(2,1)} %param.4, bf16[96,1,8,1536]{3,2,1,0:T(8,128)(2,1)S(1)} %get-tuple-element.4), kind=kOutput, calls=%fused_computation.6 | convolution fusion | flops 1811939328 | bytes 23592960 | tf_op jit(solution)/shard_map/nsk,vnk->vns/dot_general | solution.py:36
  434.8 11.3 %fusion.4 = f32[8,96,768]{2,1,0:T(8,128)} fusion(bf16[2,8,768,1536]{3,2,1,0:T(8,128)(2,1)} %param.4, bf16[96,1,8,1536]{3,2,1,0:T(8,128)(2,1)S(1)} %get-tuple-element.5), kind=kOutput, calls=%fused_computation.4 | convolution fusion | flops 1811939328 | bytes 23592960 | tf_op jit(solution)/shard_map/nsk,vnk->vns/dot_general | solution.py:39
  446.0 10.8 %fusion.88 = bf16[96,1,8,768]{3,0,2,1:T(8,128)(2,1)S(1)} fusion(f32[8,96,768]{2,1,0:T(8,128)} %fusion.6, bf16[2,8,768,1536]{3,2,1,0:T(8,128)(2,1)} %param.4, bf16[96,1,8,1536]{3,2,1,0:T(8,128)(2,1)S(1)} %get-tuple-element.5), kind=kOutput, calls=%fused_computation.86 | convolution fusion | flops 1813118976 | bytes 24772608 | tf_op jit(solution)/shard_map/nsk,vnk->vns/dot_general | solution.py:34
  456.8 10.8 %fusion.93 = bf16[96,1,8,768]{3,0,2,1:T(8,128)(2,1)S(1)} fusion(f32[8,96,768]{2,1,0:T(8,128)} %fusion.4, bf16[2,8,768,1536]{3,2,1,0:T(8,128)(2,1)} %param.4, bf16[96,1,8,1536]{3,2,1,0:T(8,128)(2,1)S(1)} %get-tuple-element.4), kind=kOutput, calls=%fused_computation.87 | convolution fusion | flops 1813118976 | bytes 24772608 | tf_op jit(solution)/shard_map/nsk,vnk->vns/dot_general | solution.py:37
  467.8 1.6 copy.35
  469.7 31.1 %reduce-scatter.15.cloned.1.call-done = bf16[24,12288]{1,0:T(8,128)(2,1)} async-done(((bf16[96,12288]{1,0:T(8,128)(2,1)}), bf16[24,12288]{1,0:T(8,128)(2,1)}) %reduce-scatter.15.cloned.1.call-update) | async-done | bytes 589840
  500.8 1.2 copy.36
  502.0 1.1 fusion.102
  503.2 1.6 fusion.75
  504.7 1.0 copy-done.2
  505.8 1.4 copy.68
  507.3 24.2 %all-gather.11.cloned.1.call-done = bf16[96,2,8,768]{3,0,2,1:T(8,128)(2,1)} async-done(((bf16[24,2,8,768]{3,0,2,1:T(8,128)(2,1)}), bf16[96,2,8,768]{3,0,2,1:T(8,128)(2,1)}) %all-gather.11.cloned.1.call-update) | async-done | bytes 2359312 | tf_op jit(solution)/shard_map/all_gather | solution.py:67
  531.4 8.4 %fusion = f32[8,96,1536]{2,1,0:T(8,128)S(1)} fusion(bf16[2,8,768,1536]{3,2,1,0:T(8,128)(2,1)} %param.4, bf16[96,2,8,768]{3,0,2,1:T(8,128)(2,1)} %all-gather.11.cloned.1.call-done), kind=kOutput, calls=%fused_computation | convolution fusion | flops 1811939328 | bytes 24772608 | tf_op jit(solution)/shard_map/nsk,vns->vnk/dot_general | solution.py:49
  539.8 8.4 %fusion.2 = f32[8,96,1536]{2,1,0:T(8,128)S(1)} fusion(bf16[2,8,768,1536]{3,2,1,0:T(8,128)(2,1)} %param.4, bf16[96,2,8,768]{3,0,2,1:T(8,128)(2,1)} %all-gather.11.cloned.1.call-done), kind=kOutput, calls=%fused_computation.2 | convolution fusion | flops 1811939328 | bytes 24772608 | tf_op jit(solution)/shard_map/nsk,vns->vnk/dot_general | solution.py:46
  548.2 8.5 %fusion.65 = bf16[96,1,8,1536]{3,0,2,1:T(8,128)(2,1)S(1)} fusion(f32[8,96,1536]{2,1,0:T(8,128)S(1)} %fusion, bf16[2,8,768,1536]{3,2,1,0:T(8,128)(2,1)} %param.4, bf16[96,2,8,768]{3,0,2,1:T(8,128)(2,1)} %all-gather.11.cloned.1.call-done), kind=kOutput, calls=%fused_computation.57 | convolution fusion | flops 1814298624 | bytes 27131904 | tf_op jit(solution)/shard_map/nsk,vns->vnk/dot_general | solution.py:47
  556.7 8.5 %fusion.62 = bf16[96,1,8,1536]{3,0,2,1:T(8,128)(2,1)S(1)} fusion(f32[8,96,1536]{2,1,0:T(8,128)S(1)} %fusion.2, bf16[2,8,768,1536]{3,2,1,0:T(8,128)(2,1)} %param.4, bf16[96,2,8,768]{3,0,2,1:T(8,128)(2,1)} %all-gather.11.cloned.1.call-done), kind=kOutput, calls=%fused_computation.56 | convolution fusion | flops 1814298624 | bytes 27131904 | tf_op jit(solution)/shard_map/nsk,vns->vnk/dot_general | solution.py:44
  565.2 0.4 pad_maximum_fusion.1
  565.6 4.7 copy.20
  570.3 95.4 %reduce-scatter.11.cloned.1.call-done = bf16[12,2,8,1536]{3,2,1,0:T(8,128)(2,1)} async-done(((bf16[96,2,8,1536]{3,2,1,0:T(8,128)(2,1)}), bf16[12,2,8,1536]{3,2,1,0:T(8,128)(2,1)}) %reduce-scatter.11.cloned.1.call-update) | async-done | bytes 589840 | tf_op jit(solution)/shard_map/reduce_scatter | solution.py:68
  665.8 2.4 fusion.68
  668.2 2.5 fusion.70
  (26 shorter events, 1.1 us)
Async XLA Ops:
  7.2 85.6 %all-gather.5.cloned.1.call-start = ((), (), s32[]{:S(2)}) async-start(), calls=%async_computation.4 | async-start | bytes 5308416 | tf_op jit(solution)/shard_map/all_gather | solution.py:54
  7.9 164.9 %reduce-scatter.13.cloned.1.call-start = ((), (), s32[]{:S(2)}) async-start(), calls=%async_computation.10 | async-start | bytes 2949120
  141.5 33.7 %copy-start.4 = (s32[24,768]{1,0:T(8,128)S(1)}, s32[24,768]{1,0:T(8,128)}, u32[]{:S(2)}) copy-start(s32[24,768]{1,0:T(8,128)} %param.6) | copy-start | bytes 221188
  141.5 60.5 %all-gather.7.cloned.1.call-start = ((), (), s32[]{:S(2)}) async-start(), calls=%async_computation.5 | async-start | bytes 2949120 | tf_op jit(solution)/shard_map/all_gather | solution.py:67
  177.8 158.5 %reduce-scatter.9.cloned.1.call-start = ((), (), s32[]{:S(2)}) async-start(), calls=%async_computation.6 | async-start | bytes 5308416 | tf_op jit(solution)/shard_map/reduce_scatter | solution.py:68
  240.8 95.5 %copy-start.3 = (s32[12,1536]{1,0:T(8,128)S(1)}, s32[12,1536]{1,0:T(8,128)}, u32[]{:S(2)}) copy-start(s32[12,1536]{1,0:T(8,128)} %param.7) | copy-start | bytes 221188
  240.9 97.9 %copy-start = (bf16[12,2,8,1536]{3,2,1,0:T(8,128)(2,1)S(1)}, bf16[12,2,8,1536]{3,2,1,0:T(8,128)(2,1)}, u32[]{:S(2)}) copy-start(bf16[12,2,8,1536]{3,2,1,0:T(8,128)(2,1)} %param.5) | copy-start | bytes 1769476
  240.9 179.9 %all-gather.9.cloned.1.call-start = ((), (), s32[]{:S(2)}) async-start(), calls=%async_computation.7 | async-start | bytes 5308416 | tf_op jit(solution)/shard_map/all_gather | solution.py:76
  341.0 159.8 %reduce-scatter.15.cloned.1.call-start = ((), (), s32[]{:S(2)}) async-start(), calls=%async_computation.11 | async-start | bytes 2949120
  469.5 62.0 %all-gather.11.cloned.1.call-start = ((), (), s32[]{:S(2)}) async-start(), calls=%async_computation.8 | async-start | bytes 2949120 | tf_op jit(solution)/shard_map/all_gather | solution.py:67
  504.7 1.0 copy-start.2
  507.2 158.5 %reduce-scatter.11.cloned.1.call-start = ((), (), s32[]{:S(2)}) async-start(), calls=%async_computation.9 | async-start | bytes 5308416 | tf_op jit(solution)/shard_map/reduce_scatter | solution.py:68
  570.3 97.9 %copy-start.1 = (bf16[12,2,8,1536]{3,2,1,0:T(8,128)(2,1)S(1)}, bf16[12,2,8,1536]{3,2,1,0:T(8,128)(2,1)}, u32[]{:S(2)}) copy-start(bf16[12,2,8,1536]{3,2,1,0:T(8,128)(2,1)} %param.5) | copy-start | bytes 1769476
Sparse Core Ops, SparseCore 0:
  10.2 82.5 all-gather.4
  141.6 31.1 reduce-scatter.12
  177.9 24.0 all-gather.6
  241.0 95.2 reduce-scatter.8
  341.1 79.6 all-gather.8
  469.6 31.1 reduce-scatter.14
  507.3 24.0 all-gather.10
  570.4 95.2 reduce-scatter.10
where the time goes:
time: 685 us; the launch traced here: 678 us
  waiting for transfers between devices  466 us (68%)
  matrix products  171 us (25%)
  local copies, waits for them, and re-layouts  23.8 us (3%)
  between operations  14.6 us (2%)
    reduce_scatter x2, waiting for transfers between devices, body(): lax.psum_scatter(adjoint_local(reflection, moving_all).astype(jnp.bfloat1...  190 us
    all_gather x1, waiting for transfers between devices, body(): initial_all = lax.all_gather(initial, 'row', axis=0, tiled=True)  84.8 us
    all_gather x1, waiting for transfers between devices, body(): lax.all_gather(plus_field.astype(jnp.bfloat16), 'row', axis=0, tiled=True)  79.7 us
    unnamed x10, waiting for transfers between devices  62.9 us
    all_gather x2, waiting for transfers between devices, body(): lax.all_gather(minus_field.astype(jnp.bfloat16), 'col', axis=0, tiled=True)  48.4 us
    dot_general x2, matrix products, forward_local(): jnp.einsum('nsk,vnk->vns', reflection[1], focus[:, 1], preferred_element_...  22.5 us
    dot_general x2, matrix products, forward_local(): jnp.einsum('nsk,vnk->vns', reflection[1], focus[:, 0], preferred_element_...  22.5 us
    dot_general x2, matrix products, forward_local(): jnp.einsum('nsk,vnk->vns', reflection[0], focus[:, 1], preferred_element_...  21.6 us
  transfers between devices with their start and end apart: 8, of which 8 were waited for; matrix products, arithmetic and copies ran while one was open for 0% of the time, Pallas kernels for 0%

commit v1 on v0

v1 whole, which is shorter than its diff:
```python
import functools
import math

import jax
import jax.numpy as jnp
from jax import lax
from jax.experimental import pallas as pl
from jax.experimental.pallas import tpu as pltpu
from jax.sharding import PartitionSpec as P

NT = 32
ITERS = 2
MESH = pl.DeviceIdType.MESH


def dft_tables(freq_count, time_count):
    time_index = lax.broadcasted_iota(jnp.int32, (time_count, freq_count), 0)
    orders = lax.broadcasted_iota(jnp.int32, (time_count, freq_count), 1) + 2
    phases = time_index * orders % time_count
    angles = phases.astype(jnp.float32) * (2.0 * math.pi / time_count)
    to_time = jnp.concatenate([jnp.cos(angles), -jnp.sin(angles)], axis=1)
    to_freq = to_time.T * (2.0 / time_count)
    return (to_time, to_freq)


def window(flattened, onsets):
    to_time, to_freq = dft_tables(flattened.shape[1] // 2, NT)
    series = jnp.einsum("tq,vqs->vts", to_time, flattened, precision=lax.Precision.HIGHEST)
    moments = lax.broadcasted_iota(jnp.int32, (1, NT, 1), 1)
    keep_mask = moments < onsets[:, None, :]
    series = jnp.where(keep_mask, series, jnp.zeros_like(series))
    return jnp.einsum("qt,vts->vqs", to_freq, series, precision=lax.Precision.HIGHEST)


def place_of(row, count):
    z, x = row // 2, row % 2
    return z + x * (count - 1 - 2 * z)


def row_of(place, count):
    half = place // (count // 2)
    return (1 - half) * 2 * place + half * (2 * (count - 1 - place) + 1)


def greet(right, left):
    barrier = pltpu.get_barrier_semaphore()
    for neighbour in (left, right):
        pl.semaphore_signal(barrier, inc=1, device_id={"row": neighbour}, device_id_type=MESH)
    pl.semaphore_wait(barrier, 2)


def chunks_of(length):
    count = 4 if length % 4 == 0 else 1
    return count, length // count


def goes(way, distance, chunk, chunks, count):
    if distance < count // 2:
        return True
    return (chunk < (chunks + 1) // 2) == (way == 0)


def gather_kernel(count, block_ref, out_ref, own_sem, send_sem, recv_sem):
    place = place_of(lax.axis_index("row"), count)
    neighbours = [row_of((place + 1) % count, count), row_of((place + count - 1) % count, count)]
    length = block_ref.shape[0]
    chunks, size = chunks_of(length)
    greet(neighbours[0], neighbours[1])
    me = lax.axis_index("row")
    own = pltpu.make_async_copy(block_ref, out_ref.at[pl.ds(me * length, length)], own_sem)
    own.start()

    started = {}
    for distance in range(1, count // 2 + 1):
        for chunk in range(chunks):
            for way in (0, 1):
                if distance > 1 and (way, distance - 1, chunk) in started:
                    started[(way, distance - 1, chunk)].wait_recv()
                if not goes(way, distance, chunk, chunks, count):
                    continue
                back = count - distance + 1 if way == 0 else distance - 1
                owner = row_of((place + back) % count, count)
                spot = pl.ds(owner * length + chunk * size, size)
                source = block_ref.at[pl.ds(chunk * size, size)] if distance == 1 else out_ref.at[spot]
                copy = pltpu.make_async_remote_copy(
                    src_ref=source,
                    dst_ref=out_ref.at[spot],
                    send_sem=send_sem.at[way, distance - 1, chunk],
                    recv_sem=recv_sem.at[way, distance - 1, chunk],
                    device_id={"row": neighbours[way]},
                    device_id_type=MESH,
                )
                copy.start()
                started[(way, distance, chunk)] = copy
    for (way, distance, chunk), copy in started.items():
        if distance == count // 2:
            copy.wait_recv()
    for copy in started.values():
        copy.wait_send()
    own.wait()


def gather_row(block, count):
    chunks, _ = chunks_of(block.shape[0])
    shape = (count * block.shape[0],) + block.shape[1:]
    return pl.pallas_call(
        functools.partial(gather_kernel, count),
        out_shape=jax.ShapeDtypeStruct(shape, block.dtype),
        in_specs=[pl.BlockSpec(memory_space=pltpu.VMEM)],
        out_specs=pl.BlockSpec(memory_space=pltpu.VMEM),
        scratch_shapes=[
            pltpu.SemaphoreType.DMA,
            pltpu.SemaphoreType.DMA((2, count // 2, chunks)),
            pltpu.SemaphoreType.DMA((2, count // 2, chunks)),
        ],
        compiler_params=pltpu.CompilerParams(
            collective_id=0, has_side_effects=True, vmem_limit_bytes=32 * 1024 * 1024
        ),
        cost_estimate=pl.CostEstimate(flops=0, bytes_accessed=16 * block.size, transcendentals=0),
    )(block)


def scatter_kernel(count, terms_ref, out_ref, held, send_sem, recv_sem):
    place = place_of(lax.axis_index("row"), count)
    neighbours = [row_of((place + 1) % count, count), row_of((place + count - 1) % count, count)]
    length = out_ref.shape[0]
    chunks, size = chunks_of(length)
    greet(neighbours[0], neighbours[1])
    me = lax.axis_index("row")

    started = {}
    for distance in range(count // 2, 0, -1):
        for chunk in range(chunks):
            for way in (0, 1):
                if not goes(way, distance, chunk, chunks, count):
                    continue
                ahead = distance if way == 0 else count - distance
                target = row_of((place + ahead) % count, count)
                term = terms_ref.at[pl.ds(target * length + chunk * size, size)]
                part = pl.ds(chunk * size, size)
                if (way, distance + 1, chunk) in started:
                    started[(way, distance + 1, chunk)].wait_recv()
                    source = held.at[way, distance, part]
                    source[...] = (source[...].astype(jnp.float32) + term[...].astype(jnp.float32)).astype(
                        source.dtype
                    )
                else:
                    source = term
                copy = pltpu.make_async_remote_copy(
                    src_ref=source,
                    dst_ref=held.at[way, distance - 1, part],
                    send_sem=send_sem.at[way, distance - 1, chunk],
                    recv_sem=recv_sem.at[way, distance - 1, chunk],
                    device_id={"row": neighbours[way]},
                    device_id_type=MESH,
                )
                copy.start()
                started[(way, distance, chunk)] = copy
    for chunk in range(chunks):
        part = pl.ds(chunk * size, size)
        total = terms_ref[pl.ds(me * length + chunk * size, size)].astype(jnp.float32)
        for way in (0, 1):
            started[(way, 1, chunk)].wait_recv()
            total += held[way, 0, part].astype(jnp.float32)
        out_ref[part] = total
    for copy in started.values():
        copy.wait_send()


def scatter_row(terms, count):
    length = terms.shape[0] // count
    chunks, _ = chunks_of(length)
    tail = terms.shape[1:]
    return pl.pallas_call(
        functools.partial(scatter_kernel, count),
        out_shape=jax.ShapeDtypeStruct((length,) + tail, jnp.float32),
        in_specs=[pl.BlockSpec(memory_space=pltpu.VMEM)],
        out_specs=pl.BlockSpec(memory_space=pltpu.VMEM),
        scratch_shapes=[
            pltpu.VMEM((2, count // 2, length) + tail, terms.dtype),
            pltpu.SemaphoreType.DMA((2, count // 2, chunks)),
            pltpu.SemaphoreType.DMA((2, count // 2, chunks)),
        ],
        compiler_params=pltpu.CompilerParams(
            collective_id=1, has_side_effects=True, vmem_limit_bytes=32 * 1024 * 1024
        ),
        cost_estimate=pl.CostEstimate(flops=0, bytes_accessed=4 * terms.size, transcendentals=0),
    )(terms)


def forward_local(reflection, focus):
    freqs = reflection.shape[1]
    parts = focus.reshape(focus.shape[0], 2, freqs, focus.shape[2])
    by_real = jnp.einsum("nsk,vonk->novs", reflection[0], parts, preferred_element_type=jnp.float32)
    by_imag = jnp.einsum("nsk,vonk->novs", reflection[1], parts, preferred_element_type=jnp.float32)
    real_part = by_real[:, 0] - by_imag[:, 1]
    imag_part = by_real[:, 1] + by_imag[:, 0]
    both = jnp.stack([real_part, imag_part], axis=0).astype(jnp.bfloat16)
    return both.reshape((2 * freqs,) + both.shape[2:]).transpose(1, 0, 2)


def adjoint_local(reflection, moving):
    freqs = reflection.shape[1]
    parts = moving.reshape(moving.shape[0], 2, freqs, moving.shape[2])
    by_real = jnp.einsum("nsk,vons->novk", reflection[0], parts, preferred_element_type=jnp.float32)
    by_imag = jnp.einsum("nsk,vons->novk", reflection[1], parts, preferred_element_type=jnp.float32)
    real_part = by_real[:, 0] + by_imag[:, 1]
    imag_part = by_real[:, 1] - by_imag[:, 0]
    both = jnp.stack([real_part, imag_part], axis=0).astype(jnp.bfloat16)
    return both.reshape((2 * freqs,) + both.shape[2:]).transpose(1, 0, 2)


def body(rows, reflection, initial, onset_down, onset_up):
    freqs = initial.shape[2]
    own = initial.reshape(initial.shape[0], 2 * freqs, initial.shape[3])
    focus_low = own
    minus_field = None
    plus_field = None
    for iteration in range(ITERS):
        focus = gather_row(focus_low, rows)
        summed = lax.psum_scatter(
            forward_local(reflection, focus), "col", scatter_dimension=0, tiled=True
        ).astype(jnp.float32)
        minus_field = window(summed, onset_down)
        moving_all = lax.all_gather(minus_field.astype(jnp.bfloat16), "col", axis=0, tiled=True)
        summed_up = scatter_row(adjoint_local(reflection, moving_all), rows)
        plus_field = own.astype(jnp.float32) + window(summed_up, onset_up)
        focus_low = plus_field.astype(jnp.bfloat16)
    return tuple(
        field.reshape(field.shape[0], 2, freqs, field.shape[2]) for field in (minus_field, plus_field)
    )


def solution(mesh):
    return jax.shard_map(
        functools.partial(body, mesh.shape["row"]),
        mesh=mesh,
        in_specs=(
            P(None, None, "row", "col"),
            P("row", None, None, "col"),
            P("col", "row"),
            P("row", "col"),
        ),
        out_specs=(P("col", None, None, "row"), P("row", None, None, "col")),
        check_vma=False,
    )
```

time: 685 us -> 529 us (0.77)
  waiting for transfers between devices: 466 us -> 113 us
  Pallas kernels: 0 us -> 196 us
  other arithmetic: 1.43 us -> 26.9 us
  matrix products: 171 us -> 151 us
    pallas_call x0 -> x4, Pallas kernels: none -> 196 us  [the longest x2 98 us: gather_row(): pl.pallas_call(functools.partial(gather_kernel, count), out_shape=jax.Sha...]
    reduce_scatter x2 -> x0, waiting for transfers between devices: 190 us -> none  [body(): lax.psum_scatter(adjoint_local(reflection, moving_all).astype(jnp.bfloat1...]
    all_gather x2 -> x0, waiting for transfers between devices: 165 us -> none  [the longest x1 84.8 us: body(): initial_all = lax.all_gather(initial, 'row', axis=0, tiled=True)]
    dot_general x16 -> x8, matrix products: 156 us -> 135 us  [the longest x2 41.7 us: forward_local(): jnp.einsum('nsk,vonk->novs', reflection[0], parts, preferred_element_type...]
    sub x0 -> x4, other arithmetic: none -> 13.5 us  [the longest x2 9.42 us: adjoint_local(): imag_part = by_real[:, 1] - by_imag[:, 0]]
    add x0 -> x4, other arithmetic: none -> 11.9 us  [the longest x2 6.44 us: adjoint_local(): real_part = by_real[:, 0] + by_imag[:, 1]]
    unnamed x14 -> x28, local copies, waits for them, and re-layouts: 6.62 us -> 16.3 us
    unnamed x10 -> x6, waiting for transfers between devices: 62.9 us -> 64.2 us
  transfers between devices with their start and end apart: 8 -> 4, of which waited for: 8 -> 4; matrix products, arithmetic and copies ran while one was open for 0% -> 0% of each run, Pallas kernels for 0% -> 0%
where the time goes in v1:
time: 529 us; the launch traced here: 523 us
  Pallas kernels  196 us (37%)
  matrix products  151 us (29%)
  waiting for transfers between devices  113 us (21%)
  other arithmetic  26.9 us (5%)
  local copies, waits for them, and re-layouts  21.5 us (4%)
  between operations  14.5 us (3%)
    pallas_call x2, Pallas kernels, gather_row(): pl.pallas_call(functools.partial(gather_kernel, count), out_shape=jax.Sha...  98 us
    pallas_call x2, Pallas kernels, scatter_row(): pl.pallas_call(functools.partial(scatter_kernel, count), out_shape=jax.Sh...  97.5 us
    unnamed x6, waiting for transfers between devices  64.2 us
    all_gather x2, waiting for transfers between devices, body(): lax.all_gather(minus_field.astype(jnp.bfloat16), 'col', axis=0, tiled=True)  48.4 us
    dot_general x2, matrix products, forward_local(): jnp.einsum('nsk,vonk->novs', reflection[0], parts, preferred_element_type...  41.7 us
    dot_general x2, matrix products, forward_local(): jnp.einsum('nsk,vonk->novs', reflection[1], parts, preferred_element_type...  41.5 us
    dot_general x2, matrix products, adjoint_local(): jnp.einsum('nsk,vons->novk', reflection[1], parts, preferred_element_type...  30.1 us
    dot_general x2, matrix products, adjoint_local(): jnp.einsum('nsk,vons->novk', reflection[0], parts, preferred_element_type...  22.1 us
  transfers between devices with their start and end apart: 4, of which 4 were waited for; matrix products, arithmetic and copies ran while one was open for 0% of the time, Pallas kernels for 0%

profile of v1, /device:TPU:0, one launch (start us, length us, event | category | flops | bytes accessed | tf_op | source)
XLA Modules:
  0.0 522.8 jit_solution(14915303703325463537)
XLA Ops:
  7.2 1.1 copy-done
  8.3 50.0 %shard_map.59 = bf16[96,16,1536]{2,1,0:T(8,128)(2,1)S(1)} custom-call(bf16[12,16,1536]{2,1,0:T(8,128)(2,1)S(1)} %bitcast.227), custom_call_target="tpu_custom_call" | custom-call | bytes 4718592 | tf_op jit(solution)/shard_map/pallas_call | solution.py:106
  58.3 2.1 copy-done.3
  60.4 20.7 %fusion.78 = f32[8,2,96,768]{3,2,0,1:T(8,128)} fusion(bf16[2,8,768,1536]{3,2,1,0:T(8,128)(2,1)} %param.4, bf16[96,2,8,1536]{3,2,1,0:T(8,128)(2,1)} %bitcast.230), kind=kOutput, calls=%fused_computation.88 | convolution fusion | flops 3623878656 | bytes 28311552 | tf_op jit(solution)/shard_map/nsk,vonk->novs/dot_general | solution.py:195
  81.1 20.8 %fusion.68 = f32[8,2,96,768]{3,2,1,0:T(8,128)} fusion(bf16[2,8,768,1536]{3,2,1,0:T(8,128)(2,1)} %param.4, bf16[96,2,8,1536]{3,2,1,0:T(8,128)(2,1)} %bitcast.231), kind=kOutput, calls=%fused_computation.86 | convolution fusion | flops 3623878656 | bytes 28311552 | tf_op jit(solution)/shard_map/nsk,vonk->novs/dot_general | solution.py:194
  101.9 2.8 fusion.91
  104.7 1.0 copy-done.6
  105.7 2.0 fusion.90
  107.9 1.6 copy.91
  109.8 33.1 %reduce-scatter.7.cloned.1.call-done = bf16[24,12288]{1,0:T(8,128)(2,1)} async-done(((bf16[96,12288]{1,0:T(8,128)(2,1)}), bf16[24,12288]{1,0:T(8,128)(2,1)}) %reduce-scatter.7.cloned.1.call-update) | async-done | bytes 589840
  142.9 1.2 copy.93
  144.1 1.1 fusion.106
  145.2 2.4 fusion.89
  147.7 24.2 %all-gather.3.cloned.1.call-done = bf16[96,16,768]{2,1,0:T(8,128)(2,1)} async-done(((bf16[24,16,768]{2,1,0:T(8,128)(2,1)}), bf16[96,16,768]{2,1,0:T(8,128)(2,1)}) %all-gather.3.cloned.1.call-update) | async-done | bytes 2359312 | tf_op jit(solution)/shard_map/all_gather | solution.py:225
  171.9 15.1 %fusion.24 = f32[8,2,96,1536]{3,2,0,1:T(8,128)} fusion(bf16[2,8,768,1536]{3,2,1,0:T(8,128)(2,1)} %param.4, bf16[96,2,8,768]{3,2,1,0:T(8,128)(2,1)} %bitcast.241), kind=kOutput, calls=%fused_computation.24 | convolution fusion | flops 3623878656 | bytes 30670848 | tf_op jit(solution)/shard_map/nsk,vons->novk/dot_general | solution.py:206
  186.9 11.1 %fusion.30 = f32[8,2,96,1536]{3,2,1,0:T(8,128)} fusion(bf16[2,8,768,1536]{3,2,1,0:T(8,128)(2,1)} %param.4, bf16[96,2,8,768]{3,2,1,0:T(8,128)(2,1)S(1)} %bitcast.242), kind=kOutput, calls=%fused_computation.26 | convolution fusion | flops 3623878656 | bytes 30670848 | tf_op jit(solution)/shard_map/nsk,vons->novk/dot_general | solution.py:205
  198.0 4.7 fusion.53
  202.8 1.7 copy-done.4
  204.5 3.2 fusion.52
  207.7 0.4 pad_maximum_fusion
  208.1 2.6 copy.122
  210.7 48.7 %shard_map.60 = f32[12,16,1536]{2,1,0:T(8,128)S(1)} custom-call(bf16[96,16,1536]{2,1,0:T(8,128)(2,1)S(1)} %bitcast.225), custom_call_target="tpu_custom_call" | custom-call | bytes 9437184 | tf_op jit(solution)/shard_map/pallas_call | solution.py:174
  259.5 2.3 fusion.47
  261.9 1.5 fusion.51.block_ref
  263.3 48.0 %shard_map.61 = bf16[96,16,1536]{2,1,0:T(8,128)(2,1)S(1)} custom-call(bf16[12,16,1536]{2,1,0:T(8,128)(2,1)S(1)} %fusion.51.block_ref), custom_call_target="tpu_custom_call" | custom-call | bytes 4718592 | tf_op jit(solution)/shard_map/pallas_call | solution.py:106
  311.4 2.1 copy-done.2
  313.5 20.8 %fusion.83 = f32[8,2,96,768]{3,2,0,1:T(8,128)} fusion(bf16[2,8,768,1536]{3,2,1,0:T(8,128)(2,1)} %param.4, bf16[96,2,8,1536]{3,2,1,0:T(8,128)(2,1)} %bitcast.228), kind=kOutput, calls=%fused_computation.89 | convolution fusion | flops 3623878656 | bytes 28311552 | tf_op jit(solution)/shard_map/nsk,vonk->novs/dot_general | solution.py:195
  334.3 20.8 %fusion.73 = f32[8,2,96,768]{3,2,1,0:T(8,128)} fusion(bf16[2,8,768,1536]{3,2,1,0:T(8,128)(2,1)} %param.4, bf16[96,2,8,1536]{3,2,1,0:T(8,128)(2,1)} %bitcast.229), kind=kOutput, calls=%fused_computation.87 | convolution fusion | flops 3623878656 | bytes 28311552 | tf_op jit(solution)/shard_map/nsk,vonk->novs/dot_general | solution.py:194
  355.2 2.8 fusion.93
  357.9 1.0 copy-done.7
  358.9 2.0 fusion.92
  361.2 1.6 copy.92
  362.8 0.3 all-gather.5.cloned.1.call-start
  363.1 31.1 %reduce-scatter.9.cloned.1.call-done = bf16[24,12288]{1,0:T(8,128)(2,1)} async-done(((bf16[96,12288]{1,0:T(8,128)(2,1)}), bf16[24,12288]{1,0:T(8,128)(2,1)}) %reduce-scatter.9.cloned.1.call-update) | async-done | bytes 589840
  394.2 1.2 copy.94
  395.3 1.1 fusion.103
  396.5 2.8 bitcast_convert_fusion
  399.3 24.2 %all-gather.5.cloned.1.call-done = bf16[96,16,768]{2,1,0:T(8,128)(2,1)} async-done(((bf16[24,16,768]{2,1,0:T(8,128)(2,1)}), bf16[96,16,768]{2,1,0:T(8,128)(2,1)}) %all-gather.5.cloned.1.call-update) | async-done | bytes 2359312 | tf_op jit(solution)/shard_map/all_gather | solution.py:225
  423.5 15.1 %fusion.27 = f32[8,2,96,1536]{3,2,0,1:T(8,128)} fusion(bf16[2,8,768,1536]{3,2,1,0:T(8,128)(2,1)} %param.4, bf16[96,2,8,768]{3,2,1,0:T(8,128)(2,1)} %bitcast.243), kind=kOutput, calls=%fused_computation.25 | convolution fusion | flops 3623878656 | bytes 30670848 | tf_op jit(solution)/shard_map/nsk,vons->novk/dot_general | solution.py:206
  438.6 11.0 %fusion.33 = f32[8,2,96,1536]{3,2,1,0:T(8,128)} fusion(bf16[2,8,768,1536]{3,2,1,0:T(8,128)(2,1)} %param.4, bf16[96,2,8,768]{3,2,1,0:T(8,128)(2,1)S(1)} %bitcast.244), kind=kOutput, calls=%fused_computation.27 | convolution fusion | flops 3623878656 | bytes 30670848 | tf_op jit(solution)/shard_map/nsk,vons->novk/dot_general | solution.py:205
  449.6 4.7 fusion.55
  454.3 1.7 copy-done.5
  456.0 3.2 fusion.54
  459.2 0.4 pad_maximum_fusion.1
  459.7 2.6 copy.121
  462.2 48.7 %shard_map.62 = f32[12,16,1536]{2,1,0:T(8,128)S(1)} custom-call(bf16[96,16,1536]{2,1,0:T(8,128)(2,1)S(1)} %bitcast.226), custom_call_target="tpu_custom_call" | custom-call | bytes 9437184 | tf_op jit(solution)/shard_map/pallas_call | solution.py:174
  511.0 2.3 fusion.46
  513.3 2.5 fusion.50
  (28 shorter events, 0.8 us)
Async XLA Ops:
  7.2 135.7 %reduce-scatter.7.cloned.1.call-start = ((), (), s32[]{:S(2)}) async-start(), calls=%async_computation.4 | async-start | bytes 2949120
  7.2 1.1 copy-start
  58.3 2.1 copy-start.3
  101.9 3.8 copy-start.6
  109.6 35.6 %copy-start.9 = (s32[24,768]{1,0:T(8,128)S(1)}, s32[24,768]{1,0:T(8,128)}, u32[]{:S(2)}) copy-start(s32[24,768]{1,0:T(8,128)} %param.6) | copy-start | bytes 221188
  109.6 62.3 %all-gather.3.cloned.1.call-start = ((), (), s32[]{:S(2)}) async-start(), calls=%async_computation.2 | async-start | bytes 2949120 | tf_op jit(solution)/shard_map/all_gather | solution.py:225
  147.6 246.5 %reduce-scatter.9.cloned.1.call-start = ((), (), s32[]{:S(2)}) async-start(), calls=%async_computation.5 | async-start | bytes 2949120
  171.9 15.1 %copy-start.10 = (bf16[96,16,768]{2,1,0:T(8,128)(2,1)S(1)}, bf16[96,16,768]{2,1,0:T(8,128)(2,1)}, u32[]{:S(2)}) copy-start(bf16[96,16,768]{2,1,0:T(8,128)(2,1)} %all-gather.3.cloned.1.call-done) | copy-start | bytes 7077892
  198.0 6.4 %copy-start.4 = (f32[8,2,96,1536]{3,2,0,1:T(8,128)S(1)}, f32[8,2,96,1536]{3,2,0,1:T(8,128)}, u32[]{:S(2)}) copy-start(f32[8,2,96,1536]{3,2,0,1:T(8,128)} %fusion.24) | copy-start | bytes 28311556
  210.7 48.8 %copy-start.8 = (s32[12,1536]{1,0:T(8,128)S(1)}, s32[12,1536]{1,0:T(8,128)}, u32[]{:S(2)}) copy-start(s32[12,1536]{1,0:T(8,128)} %param.7) | copy-start | bytes 221188
  259.5 2.4 copy-start.1
  311.4 2.1 copy-start.2
  355.2 3.8 copy-start.7
  362.8 60.7 %all-gather.5.cloned.1.call-start = ((), (), s32[]{:S(2)}) async-start(), calls=%async_computation.3 | async-start | bytes 2949120 | tf_op jit(solution)/shard_map/all_gather | solution.py:225
  423.5 15.1 %copy-start.11 = (bf16[96,16,768]{2,1,0:T(8,128)(2,1)S(1)}, bf16[96,16,768]{2,1,0:T(8,128)(2,1)}, u32[]{:S(2)}) copy-start(bf16[96,16,768]{2,1,0:T(8,128)(2,1)} %all-gather.5.cloned.1.call-done) | copy-start | bytes 7077892
  449.5 6.4 %copy-start.5 = (f32[8,2,96,1536]{3,2,0,1:T(8,128)S(1)}, f32[8,2,96,1536]{3,2,0,1:T(8,128)}, u32[]{:S(2)}) copy-start(f32[8,2,96,1536]{3,2,0,1:T(8,128)} %fusion.27) | copy-start | bytes 28311556
Sparse Core Ops, SparseCore 0:
  109.7 33.1 reduce-scatter.6
  147.8 24.0 all-gather.2
  362.9 31.1 reduce-scatter.8
  399.4 24.0 all-gather.4
